TPU v7x, 32 devices: a whole 2x2x4 slice. The times are simulated.
32 devices in a mesh: strike: 8 (over z, x), dip: 4 (over y, core).
Axes of the slice: x: 2, y: 2, z: 4, core: 2. Of those that a mesh axis runs over, the one named last changes fastest.
Arguments:
- pressure: float32 [64, 512, 512], P(None, 'strike', 'dip'), may hold values from -6 to 6
- strike_vel: float32 [64, 512, 512], P(None, 'strike', 'dip'), may hold values from -6 to 6
- dip_vel: float32 [64, 512, 512], P(None, 'strike', 'dip'), may hold values from -6 to 6
- bathy_class: int32 [512, 512], P('strike', 'dip'), may hold values from 0 to 7
- bulk_table: float32 [8], replicated, may hold values from 0.5 to 2
- buoy_table: float32 [8], replicated, may hold values from 0.5 to 2
- gravity: float32 [64], replicated, may hold values from 0.5 to 2
- sensor_amp: float32 [4, 256], P(None, ('strike', 'dip')), may hold values from -12 to 12
- sensor_owner: int32 [256, 1], P(('strike', 'dip')), may hold values from 0 to 3; in each aligned block of 8 rows (0 to 7, 8 to 15, ...) at most 2 rows name the same one
- sensor_cell: int32 [256], P(('strike', 'dip')), may hold values from 0 to 8191
- probe_kernel: bfloat16 [96, 512, 512], P(None, 'strike', 'dip'), may hold values from -6 to 6
Outputs:
- final_pressure: float32 [64, 512, 512], P(None, 'strike', 'dip')
- panel_factor: float32 [96, 96], replicated
Inputs may be any that keep to these rules, and one draw needn't show every extreme that they name: `sensor_owner`: the owner lies in the same strike index as the device that holds the sensor; among the 8 sensors of one device at most 2 name the same owner, a bound that some block reaches. `sensor_cell`: numbered row by row within the owner's block, 128 cells a row.
All inputs are finite; a program needn't handle non-finite values.
Results may differ from a plain program's by a relative error of at most 0.0003.
Values sent between devices are 32-bit elements; how exact they have to be, the bound alone decides.
A program may use at most 128 MiB of HBM per device.

v0:
```python
import math

import jax
import jax.numpy as jnp
from jax import lax
from jax.sharding import PartitionSpec as P

STEPS = 4
PROBES = 96
NCLASS = 8
CAP = 2


time_step = 0.2


def extended_2(shard, sides, width):
    for axis, dim in sides:
        devices, length = (lax.axis_size(axis), shard.shape[dim])
        up = [(i, (i + 1) % devices) for i in range(devices - 1)]
        down = [(j, i) for i, j in up]
        last = lax.slice_in_dim(shard, length - width, length, axis=dim)
        initial = lax.slice_in_dim(shard, 0, width, axis=dim)
        before = lax.ppermute(last, axis, up)
        after = lax.ppermute(initial, axis, down)
        shard = jnp.concatenate([before, shard, after], axis=dim)
    return shard


def fourth_diff(extended, axis):
    length = extended.shape[axis] - 4

    def window(offset):
        return lax.slice_in_dim(extended, offset, offset + length, axis=axis)

    return (8.0 * (window(3) - window(1)) - (window(4) - window(0))) / 12.0


def pad_axis(field, axis, width):
    widths = [(0, 0)] * field.ndim
    widths[axis] = (width, width)
    return jnp.pad(field, widths)


def depth_diff(field):
    padded = pad_axis(field, 0, 1)
    return (padded[2:] - padded[:-2]) / 2.0


def lookup(classes, table):
    labels = jnp.arange(NCLASS, dtype=jnp.int32)[:, None, None]
    return jnp.sum(jnp.where(classes[None] == labels, table[:, None, None], 0.0), axis=0)


def advance(
    pressure,
    strike_vel,
    dip_vel,
    vertical,
    bulk,
    buoy,
    gravity,
    inject_now,
    grow_both,
    grow_strike,
    grow_dip,
):
    extended = grow_both(pressure)
    strike_vel = strike_vel - time_step * buoy * fourth_diff(extended[:, :, 2:-2], 1)
    dip_vel = dip_vel - time_step * buoy * fourth_diff(extended[:, 2:-2, :], 2)
    vertical = vertical - time_step * buoy * depth_diff(pressure)
    divergence = (
        fourth_diff(grow_strike(strike_vel), 1)
        + fourth_diff(grow_dip(dip_vel), 2)
        + depth_diff(vertical)
    )
    pressure = (
        pressure - time_step * bulk * divergence + time_step * gravity[:, None, None] * vertical
    )
    pressure = pressure.at[-1].add(inject_now)
    return (pressure, strike_vel, dip_vel, vertical)


def rim_pressure(field):
    return extended_2(field, (("strike", 1), ("dip", 2)), 2)


def rim_strike(field):
    return extended_2(field, (("strike", 1),), 2)


def rim_dip(field):
    return extended_2(field, (("dip", 2),), 2)


def body(
    pressure,
    strike_vel,
    dip_vel,
    bathy_class,
    bulk_table,
    buoy_table,
    gravity,
    sensor_amp,
    sensor_owner,
    sensor_cell,
    probe_kernel,
):
    levels, rows_x, rows_y = pressure.shape
    cells = rows_x * rows_y
    bulk = lookup(bathy_class, bulk_table)
    buoy = lookup(bathy_class, buoy_table)
    cell_float = sensor_cell.astype(jnp.float32)
    cell_labels = jnp.arange(cells, dtype=jnp.float32)[None]
    owners = sensor_owner[:, 0]
    dip_count = lax.axis_size("dip")
    slot_count = dip_count * CAP
    member = (owners[:, None] == jnp.arange(dip_count, dtype=jnp.int32)[None]).astype(jnp.float32)
    before = jnp.sum((jnp.cumsum(member, axis=0) - member) * member, axis=1)
    slot = owners.astype(jnp.float32) * CAP + before
    placing = (slot[:, None] == jnp.arange(slot_count, dtype=jnp.float32)[None]).astype(jnp.float32)
    sent_amp = jnp.dot(sensor_amp, placing, precision=lax.Precision.HIGHEST)
    sent_cell = jnp.dot((cell_float + 1.0)[None], placing, precision=lax.Precision.HIGHEST) - 1.0
    got_amp, got_cell = (
        lax.all_to_all(sent_amp, "dip", split_axis=1, concat_axis=1, tiled=True),
        lax.all_to_all(sent_cell, "dip", split_axis=1, concat_axis=1, tiled=True),
    )
    selector = (got_cell[0][:, None] == cell_labels).astype(jnp.float32)
    inject = jnp.dot(got_amp, selector, precision=lax.Precision.HIGHEST).reshape(
        STEPS, rows_x, rows_y
    )
    vertical = jnp.zeros_like(pressure)
    for step in range(STEPS):
        pressure, strike_vel, dip_vel, vertical = advance(
            pressure,
            strike_vel,
            dip_vel,
            vertical,
            bulk,
            buoy,
            gravity,
            inject[step],
            rim_pressure,
            rim_strike,
            rim_dip,
        )
    seafloor = pressure[-1]
    total_cells = cells * lax.axis_size("strike") * lax.axis_size("dip")
    scale = 1.0 / math.sqrt(total_cells)
    panel = (probe_kernel.astype(jnp.float32) * seafloor[None] * scale).reshape(PROBES, cells)
    gram = jnp.dot(panel, panel.T, precision=lax.Precision.HIGHEST)
    total_gram = lax.psum(gram, ("strike", "dip"))
    panel_factor = jnp.linalg.cholesky(total_gram).T
    return (pressure, panel_factor)


def solution(mesh):
    return jax.shard_map(
        body,
        mesh=mesh,
        in_specs=(
            P(None, "strike", "dip"),
            P(None, "strike", "dip"),
            P(None, "strike", "dip"),
            P("strike", "dip"),
            P(),
            P(),
            P(),
            P(None, ("strike", "dip")),
            P(("strike", "dip"), None),
            P(("strike", "dip")),
            P(None, "strike", "dip"),
        ),
        out_specs=(P(None, "strike", "dip"), P()),
        check_vma=False,
    )
```

profile of v0, /device:TPU:0, one launch (start us, length us, event | category | flops | bytes accessed | tf_op | source)
XLA Modules:
  0.0 432.5 jit_solution(11149279473837441230)
XLA Ops:
  3.6 4.8 %collective-permute-start.1 = (f32[64,2,128]{2,0,1:T(8,128)S(1)}, f32[64,2,128]{2,0,1:T(8,128)S(1)}, u32[]{:S(2)}, u32[]{:S(2)}) collective-permute-start(f32[64,2,128]{2,0,1:T(8,128)S(1)} %get-tuple-element.102), channel_id=1, source_target_pairs={{0,4},{4,8},{8,12},{12,16},{16,20},{20,24},{24,28},{1,5},{5,9},{9,... | collective-permute-start | bytes 196616 | tf_op jit(solution)/shard_map/ppermute | solution.py:24
  10.8 3.2 all-to-all-start.1
  17.9 3.4 fusion.163
  28.3 3.0 collective-permute-start.5
  32.0 3.5 all-to-all-start
  36.7 3.1 copy.107
  39.9 3.1 copy.109
  43.0 11.6 %fusion.135 = (f32[64,64,128]{2,0,1:T(8,128)S(1)}, f32[64,64,128]{2,0,1:T(8,128)}) fusion(f32[64,68,128]{2,0,1:T(8,128)S(1)} %get-tuple-element.103, f32[64,68,2]{2,0,1:T(8,128)} %copy.109, f32[64,68,2]{2,0,1:T(8,128)} %copy.107, f32[64,64,128]{2,1,0:T(8,128)} %param.21, f32[64,128]{1,0:T(8,128)S(1)} %get-tuple-element.110, f32[64,66,128]{2,0,1:T(8,128)} %copy-done.18, ...), kind=kLoop, calls=%fused_computation.241 | loop fusion | flops 8388608 | bytes 19107840 | tf_op jit(solution)/shard_map/sub | solution.py:70
  61.9 4.2 collective-permute-start.7
  68.3 5.4 %collective-permute-start.3 = (f32[64,2,128]{2,0,1:T(8,128)S(1)}, f32[64,2,128]{2,0,1:T(8,128)S(1)}, u32[]{:S(2)}, u32[]{:S(2)}) collective-permute-start(f32[64,2,128]{2,0,1:T(8,128)S(1)} %get-tuple-element.100), channel_id=1, source_target_pairs={{0,4},{4,8},{8,12},{12,16},{16,20},{20,24},{24,28},{1,5},{5,9},{9,... | collective-permute-start | bytes 196616 | tf_op jit(solution)/shard_map/ppermute | solution.py:24
  80.0 16.9 %fusion.65 = f32[64,64,128]{2,0,1:T(8,128)S(1)} fusion(f32[64,2,128]{2,0,1:T(8,128)S(1)} %collective-permute-done.3, f32[64,64,128]{2,0,1:T(8,128)} %get-tuple-element.108, f32[64,2,128]{2,0,1:T(8,128)S(1)} %collective-permute-done.2, f32[64,64,128]{2,0,1:T(8,128)} %fusion.69, f32[64,64,2]{2,0,1:T(8,128)} %copy.114, f32[64,64,128]{2,0,1:T(8,128)} %copy-done.6, ...), kind=kLoop, calls=%fused_computation.129 | loop fusion | flops 13107200 | bytes 10715392 | tf_op jit(solution)/shard_map/add | solution.py:78
  98.5 5.4 %collective-permute-start.9 = (f32[64,2,128]{2,0,1:T(8,128)S(1)}, f32[64,2,128]{2,0,1:T(8,128)S(1)}, u32[]{:S(2)}, u32[]{:S(2)}) collective-permute-start(f32[64,2,128]{2,0,1:T(8,128)S(1)} %get-tuple-element.93), channel_id=1, source_target_pairs={{0,4},{4,8},{8,12},{12,16},{16,20},{20,24},{24,28},{1,5},{5,9},{9,... | collective-permute-start | bytes 196616 | tf_op jit(solution)/shard_map/ppermute | solution.py:24
  106.9 3.0 fusion.162
  116.8 3.0 collective-permute-start.13
  119.9 7.2 %fusion.74 = (f32[64,64,128]{2,0,1:T(8,128)}, f32[64,64,128]{2,0,1:T(8,128)S(1)}) fusion(f32[64,64,128]{2,0,1:T(8,128)S(1)} %scatter-add.14, f32[64,128]{1,0:T(8,128)S(1)} %get-tuple-element.109, f32[64,64,128]{2,0,1:T(8,128)} %get-tuple-element.108, f32[64,128]{1,0:T(8,128)S(1)} %get-tuple-element.110, f32[64,2,128]{2,0,1:T(8,128)S(1)} %collective-permute-done.9, ...), kind=kLoop, calls=%fused_computation.138 | loop fusion | flops 8388608 | bytes 10682368 | tf_op jit(solution)/shard_map/sub | solution.py:71
  129.8 5.5 %collective-permute-start.11 = (f32[64,2,128]{2,0,1:T(8,128)S(1)}, f32[64,2,128]{2,0,1:T(8,128)S(1)}, u32[]{:S(2)}, u32[]{:S(2)}) collective-permute-start(f32[64,2,128]{2,0,1:T(8,128)S(1)} %get-tuple-element.91), channel_id=1, source_target_pairs={{0,4},{4,8},{8,12},{12,16},{16,20},{20,24},{24,28},{1,5},{5,9},{9,... | collective-permute-start | bytes 196616 | tf_op jit(solution)/shard_map/ppermute | solution.py:24
  135.3 3.1 copy.121
  138.5 3.1 copy.123
  141.6 6.9 %fusion.127 = f32[64,64,128]{2,0,1:T(8,128)S(1)} fusion(f32[64,64,128]{2,0,1:T(8,128)} %copy-done.6, f32[64,68,2]{2,0,1:T(8,128)} %copy.123, f32[64,2,128]{2,0,1:T(8,128)S(1)} %collective-permute-done.8, f32[64,64,128]{2,0,1:T(8,128)S(1)} %scatter-add.14, f32[64,2,128]{2,0,1:T(8,128)S(1)} %collective-permute-done.9, f32[64,68,2]{2,0,1:T(8,128)} %copy.121, ...), kind=kLoop, calls=%fused_computation.220 | loop fusion | flops 9437184 | bytes 6524928 | tf_op jit(solution)/shard_map/sub | solution.py:70
  157.9 3.8 collective-permute-start.15
  167.6 15.8 %fusion.47 = f32[64,64,128]{2,0,1:T(8,128)S(1)} fusion(f32[64,64,128]{2,0,1:T(8,128)S(1)} %scatter-add.14, f32[64,2,128]{2,0,1:T(8,128)S(1)} %collective-permute-done.11, f32[64,64,128]{2,0,1:T(8,128)} %copy-done.12, f32[64,2,128]{2,0,1:T(8,128)S(1)} %collective-permute-done.10, f32[64,64,128]{2,0,1:T(8,128)} %get-tuple-element.88, f32[64,64,2]{2,0,1:T(8,128)} %copy.127, ...), kind=kLoop, calls=%fused_computation.111 | loop fusion | flops 13107200 | bytes 10715392 | tf_op jit(solution)/shard_map/add | solution.py:78
  188.7 5.8 %collective-permute-start.17 = (f32[64,2,128]{2,0,1:T(8,128)S(1)}, f32[64,2,128]{2,0,1:T(8,128)S(1)}, u32[]{:S(2)}, u32[]{:S(2)}) collective-permute-start(f32[64,2,128]{2,0,1:T(8,128)S(1)} %get-tuple-element.85), channel_id=1, source_target_pairs={{0,4},{4,8},{8,12},{12,16},{16,20},{20,24},{24,28},{1,5},{5,9},{9,... | collective-permute-start | bytes 196616 | tf_op jit(solution)/shard_map/ppermute | solution.py:24
  199.0 3.0 fusion.161
  202.0 3.0 copy.129
  209.1 3.0 collective-permute-start.21
  212.1 5.5 %fusion.79 = (f32[64,64,128]{2,0,1:T(8,128)}, f32[64,64,128]{2,0,1:T(8,128)S(1)}) fusion(f32[64,64,128]{2,0,1:T(8,128)} %get-tuple-element.88, f32[64,64,128]{2,0,1:T(8,128)S(1)} %copy-done.3, f32[64,128]{1,0:T(8,128)S(1)} %get-tuple-element.109, f32[64,64,128]{2,0,1:T(8,128)} %copy-done.12, f32[64,128]{1,0:T(8,128)S(1)} %get-tuple-element.110, ...), kind=kLoop, calls=%fused_computation.143 | loop fusion | flops 6815744 | bytes 10682368 | tf_op jit(solution)/shard_map/sub | solution.py:71
  220.3 5.2 %collective-permute-start.19 = (f32[64,2,128]{2,0,1:T(8,128)S(1)}, f32[64,2,128]{2,0,1:T(8,128)S(1)}, u32[]{:S(2)}, u32[]{:S(2)}) collective-permute-start(f32[64,2,128]{2,0,1:T(8,128)S(1)} %get-tuple-element.83), channel_id=1, source_target_pairs={{0,4},{4,8},{8,12},{12,16},{16,20},{20,24},{24,28},{1,5},{5,9},{9,... | collective-permute-start | bytes 196616 | tf_op jit(solution)/shard_map/ppermute | solution.py:24
  225.5 3.1 copy.130
  228.7 3.1 copy.132
  231.8 6.9 %fusion.119 = f32[64,64,128]{2,0,1:T(8,128)S(1)} fusion(f32[64,64,128]{2,0,1:T(8,128)} %copy-done.8, f32[64,68,2]{2,0,1:T(8,128)} %copy.132, f32[64,2,128]{2,0,1:T(8,128)S(1)} %collective-permute-done.16, f32[64,64,128]{2,0,1:T(8,128)S(1)} %copy-done.3, f32[64,2,128]{2,0,1:T(8,128)S(1)} %collective-permute-done.17, f32[64,68,2]{2,0,1:T(8,128)} %copy.130, ...), kind=kLoop, calls=%fused_computation.199 | loop fusion | flops 9437184 | bytes 6524928 | tf_op jit(solution)/shard_map/sub | solution.py:70
  248.1 4.2 collective-permute-start.23
  258.2 15.8 %fusion.29 = f32[64,64,128]{2,0,1:T(8,128)S(1)} fusion(f32[64,64,128]{2,0,1:T(8,128)S(1)} %copy-done.3, f32[64,2,128]{2,0,1:T(8,128)S(1)} %collective-permute-done.19, f32[64,64,128]{2,0,1:T(8,128)} %copy-done.11, f32[64,2,128]{2,0,1:T(8,128)S(1)} %collective-permute-done.18, f32[64,64,128]{2,0,1:T(8,128)} %get-tuple-element.80, f32[64,64,2]{2,0,1:T(8,128)} %copy.136, ...), kind=kLoop, calls=%fused_computation.93 | loop fusion | flops 13107200 | bytes 10715392 | tf_op jit(solution)/shard_map/add | solution.py:78
  279.4 5.6 %collective-permute-start.25 = (f32[64,2,128]{2,0,1:T(8,128)S(1)}, f32[64,2,128]{2,0,1:T(8,128)S(1)}, u32[]{:S(2)}, u32[]{:S(2)}) collective-permute-start(f32[64,2,128]{2,0,1:T(8,128)S(1)} %get-tuple-element.77), channel_id=1, source_target_pairs={{0,4},{4,8},{8,12},{12,16},{16,20},{20,24},{24,28},{1,5},{5,9},{9,... | collective-permute-start | bytes 196616 | tf_op jit(solution)/shard_map/ppermute | solution.py:24
  289.5 3.0 fusion.160
  292.4 3.0 copy.138
  299.5 3.0 collective-permute-start.29
  302.6 5.5 %fusion.84 = (f32[64,64,128]{2,0,1:T(8,128)}, f32[64,64,128]{2,0,1:T(8,128)S(1)}) fusion(f32[64,64,128]{2,0,1:T(8,128)} %get-tuple-element.80, f32[64,64,128]{2,0,1:T(8,128)S(1)} %copy-done.5, f32[64,128]{1,0:T(8,128)S(1)} %get-tuple-element.109, f32[64,64,128]{2,0,1:T(8,128)} %copy-done.11, f32[64,128]{1,0:T(8,128)S(1)} %get-tuple-element.110, ...), kind=kLoop, calls=%fused_computation.148 | loop fusion | flops 6815744 | bytes 10682368 | tf_op jit(solution)/shard_map/sub | solution.py:71
  310.7 5.5 %collective-permute-start.27 = (f32[64,2,128]{2,0,1:T(8,128)S(1)}, f32[64,2,128]{2,0,1:T(8,128)S(1)}, u32[]{:S(2)}, u32[]{:S(2)}) collective-permute-start(f32[64,2,128]{2,0,1:T(8,128)S(1)} %get-tuple-element.75), channel_id=1, source_target_pairs={{0,4},{4,8},{8,12},{12,16},{16,20},{20,24},{24,28},{1,5},{5,9},{9,... | collective-permute-start | bytes 196616 | tf_op jit(solution)/shard_map/ppermute | solution.py:24
  316.2 3.1 copy.139
  319.4 3.1 copy.141
  322.5 6.9 %fusion.111 = f32[64,64,128]{2,0,1:T(8,128)S(1)} fusion(f32[64,64,128]{2,0,1:T(8,128)} %copy-done.7, f32[64,68,2]{2,0,1:T(8,128)} %copy.141, f32[64,2,128]{2,0,1:T(8,128)S(1)} %collective-permute-done.24, f32[64,64,128]{2,0,1:T(8,128)S(1)} %copy-done.5, f32[64,2,128]{2,0,1:T(8,128)S(1)} %collective-permute-done.25, f32[64,68,2]{2,0,1:T(8,128)} %copy.139, ...), kind=kLoop, calls=%fused_computation.178 | loop fusion | flops 9437184 | bytes 6524928 | tf_op jit(solution)/shard_map/sub | solution.py:70
  329.4 3.0 fusion.164
  339.0 4.1 collective-permute-start.31
  343.1 3.0 copy.143
  349.0 15.4 %fusion.11 = f32[64,64,128]{2,0,1:T(8,128)S(1)} fusion(f32[64,64,128]{2,0,1:T(8,128)S(1)} %copy-done.5, f32[64,2,128]{2,0,1:T(8,128)S(1)} %collective-permute-done.27, f32[64,64,128]{2,0,1:T(8,128)} %copy-done.15, f32[64,2,128]{2,0,1:T(8,128)S(1)} %collective-permute-done.26, f32[64,64,128]{2,0,1:T(8,128)} %get-tuple-element.72, f32[64,64,2]{2,0,1:T(8,128)} %copy.145, ...), kind=kLoop, calls=%fused_computation.75 | loop fusion | flops 13107200 | bytes 10715392 | tf_op jit(solution)/shard_map/add | solution.py:78
  369.5 6.0 %fusion.142 = f32[96,96]{0,1:T(8,128)S(1)} fusion(f32[96,64,128]{2,1,0:T(8,128)S(1)} %multiply_multiply_fusion), kind=kOutput, calls=%fused_computation.254 | convolution fusion | flops 905969664 | bytes 3182592 | tf_op jit(solution)/shard_map/dot_general | solution.py:151
  375.5 43.3 %psum.7 = f32[96,96]{0,1:T(8,128)S(1)} all-reduce(f32[96,96]{0,1:T(8,128)S(1)} %fusion.142), channel_id=1, replica_groups=mesh['strike'=8,'dip'=4] {'strike','dip'}, use_global_device_ids=true, to_apply=%region_4.5 | all-reduce | flops 9216 | bytes 73728 | tf_op jit(solution)/shard_map/psum | solution.py:152
  418.9 8.8 %cholesky.18 = f32[96,96]{1,0:T(8,128)S(1)} custom-call(f32[96,96]{1,0:T(8,128)S(1)} %fusion.148), custom_call_target="Cholesky" | custom-call | tf_op jit(solution)/shard_map/jit(cholesky)/cholesky | solution.py:153
  (172 shorter events, 130.6 us)
Async XLA Ops:
  0.6 15.6 %copy-start = (f32[4,8]{1,0:T(4,128)S(1)}, f32[4,8]{1,0:T(4,128)}, u32[]{:S(2)}) copy-start(f32[4,8]{1,0:T(4,128)} %param.26) | copy-start | bytes 388
  0.6 9.1 %copy-start.20 = (s32[8,1]{0,1:T(1,128)S(1)}, s32[8,1]{0,1:T(1,128)}, u32[]{:S(2)}) copy-start(s32[8,1]{0,1:T(1,128)} %param.27) | copy-start | bytes 100
  0.7 9.3 %copy-start.23 = (s32[8]{0:T(128)S(1)}, s32[8]{0:T(128)}, u32[]{:S(2)}) copy-start(s32[8]{0:T(128)} %param.28) | copy-start | bytes 100
  0.7 13.4 %copy-start.19 = (s32[64,128]{1,0:T(8,128)S(1)}, s32[64,128]{1,0:T(8,128)}, u32[]{:S(2)}) copy-start(s32[64,128]{1,0:T(8,128)} %param.22) | copy-start | bytes 98308
  0.7 13.4 %copy-start.21 = (f32[8]{0:T(128)S(1)}, f32[8]{0:T(128)}, u32[]{:S(2)}) copy-start(f32[8]{0:T(128)} %param.23) | copy-start | bytes 100
  0.7 13.4 %copy-start.22 = (f32[8]{0:T(128)S(1)}, f32[8]{0:T(128)}, u32[]{:S(2)}) copy-start(f32[8]{0:T(128)} %param.24) | copy-start | bytes 100
  3.5 12.7 %copy-start.10 = (f32[64,64,128]{2,0,1:T(8,128)}, f32[64,64,128]{2,0,1:T(8,128)S(1)}, u32[]{:S(2)}) copy-start(f32[64,64,128]{2,0,1:T(8,128)S(1)} %copy.116) | copy-start | bytes 6291460
  3.6 12.9 %collective-permute-start.1 = (f32[64,2,128]{2,0,1:T(8,128)S(1)}, f32[64,2,128]{2,0,1:T(8,128)S(1)}, u32[]{:S(2)}, u32[]{:S(2)}) collective-permute-start(f32[64,2,128]{2,0,1:T(8,128)S(1)} %get-tuple-element.102), channel_id=1, source_target_pairs={{0,4},{4,8},{8,12},{12,16},{16,20},{20,24},{24,28},{1,5},{5,9},{9,... | collective-permute-start | bytes 196616 | tf_op jit(solution)/shard_map/ppermute | solution.py:24
  8.4 9.4 %collective-permute-start = (f32[64,2,128]{2,0,1:T(8,128)S(1)}, f32[64,2,128]{2,0,1:T(8,128)S(1)}, u32[]{:S(2)}, u32[]{:S(2)}) collective-permute-start(f32[64,2,128]{2,0,1:T(8,128)S(1)} %get-tuple-element.101), channel_id=1, source_target_pairs={{4,0},{8,4},{12,8},{16,12},{20,16},{24,20},{28,24},{5,1},{9,5},{13... | collective-permute-start | bytes 196616 | tf_op jit(solution)/shard_map/ppermute | solution.py:25
  10.8 21.2 %all-to-all-start.1 = ((f32[1,4,2]{2,0,1:T(1,128)}), f32[1,4,2]{2,0,1:T(1,128)S(1)}, u32[]{:S(2)}, u32[]{:S(2)}) async-start(f32[1,4,2]{2,0,1:T(1,128)} %bitcast.8), calls=%async_computation.1 | async-start | bytes 4096 | tf_op jit(solution)/shard_map/all_to_all | solution.py:126
  17.8 3.5 copy-start.18
  17.9 3.5 copy-start.14
  21.3 10.0 %copy-start.24 = (f32[64]{0:T(128)S(1)}, f32[64]{0:T(128)}, u32[]{:S(2)}) copy-start(f32[64]{0:T(128)} %param.25) | copy-start | bytes 772
  24.2 12.6 %collective-permute-start.4 = (f32[64,68,2]{1,0,2:T(8,128)S(1)}, f32[64,68,2]{1,0,2:T(8,128)S(1)}, u32[]{:S(2)}, u32[]{:S(2)}) collective-permute-start(f32[64,68,2]{1,0,2:T(8,128)S(1)} %copy.106), channel_id=1, source_target_pairs={{1,0},{2,1},{3,2},{5,4},{6,5},{7,6},{9,8},{10,9},{11,10},{13,12},{... | collective-permute-start | bytes 104456 | tf_op jit(solution)/shard_map/ppermute | solution.py:25
  28.3 11.6 %collective-permute-start.5 = (f32[64,68,2]{1,0,2:T(8,128)S(1)}, f32[64,68,2]{1,0,2:T(8,128)S(1)}, u32[]{:S(2)}, u32[]{:S(2)}) collective-permute-start(f32[64,68,2]{1,0,2:T(8,128)S(1)} %copy.108), channel_id=1, source_target_pairs={{0,1},{1,2},{2,3},{4,5},{5,6},{6,7},{8,9},{9,10},{10,11},{12,13},{... | collective-permute-start | bytes 104456 | tf_op jit(solution)/shard_map/ppermute | solution.py:24
  32.0 41.8 %all-to-all-start = ((f32[4,4,2]{0,2,1:T(2,128)}), f32[4,4,2]{0,2,1:T(2,128)S(1)}, u32[]{:S(2)}, u32[]{:S(2)}) async-start(f32[4,4,2]{0,2,1:T(2,128)} %bitcast.4), calls=%async_computation | async-start | bytes 8192 | tf_op jit(solution)/shard_map/all_to_all | solution.py:125
  59.3 14.8 %collective-permute-start.6 = (f32[64,64,2]{1,0,2:T(8,128)S(1)}, f32[64,64,2]{1,0,2:T(8,128)S(1)}, u32[]{:S(2)}, u32[]{:S(2)}) collective-permute-start(f32[64,64,2]{1,0,2:T(8,128)S(1)} %copy.111), channel_id=1, source_target_pairs={{1,0},{2,1},{3,2},{5,4},{6,5},{7,6},{9,8},{10,9},{11,10},{13,12},{... | collective-permute-start | bytes 98312 | tf_op jit(solution)/shard_map/ppermute | solution.py:25
  61.9 15.1 %collective-permute-start.7 = (f32[64,64,2]{1,0,2:T(8,128)S(1)}, f32[64,64,2]{1,0,2:T(8,128)S(1)}, u32[]{:S(2)}, u32[]{:S(2)}) collective-permute-start(f32[64,64,2]{1,0,2:T(8,128)S(1)} %copy.113), channel_id=1, source_target_pairs={{0,1},{1,2},{2,3},{4,5},{5,6},{6,7},{8,9},{9,10},{10,11},{12,13},{... | collective-permute-start | bytes 98312 | tf_op jit(solution)/shard_map/ppermute | solution.py:24
  67.0 13.0 %collective-permute-start.2 = (f32[64,2,128]{2,0,1:T(8,128)S(1)}, f32[64,2,128]{2,0,1:T(8,128)S(1)}, u32[]{:S(2)}, u32[]{:S(2)}) collective-permute-start(f32[64,2,128]{2,0,1:T(8,128)S(1)} %get-tuple-element.99), channel_id=1, source_target_pairs={{4,0},{8,4},{12,8},{16,12},{20,16},{24,20},{28,24},{5,1},{9,5},{13... | collective-permute-start | bytes 196616 | tf_op jit(solution)/shard_map/ppermute | solution.py:25
  68.3 11.7 %collective-permute-start.3 = (f32[64,2,128]{2,0,1:T(8,128)S(1)}, f32[64,2,128]{2,0,1:T(8,128)S(1)}, u32[]{:S(2)}, u32[]{:S(2)}) collective-permute-start(f32[64,2,128]{2,0,1:T(8,128)S(1)} %get-tuple-element.100), channel_id=1, source_target_pairs={{0,4},{4,8},{8,12},{12,16},{16,20},{20,24},{24,28},{1,5},{5,9},{9,... | collective-permute-start | bytes 196616 | tf_op jit(solution)/shard_map/ppermute | solution.py:24
  97.2 7.3 %collective-permute-start.8 = (f32[64,2,128]{2,0,1:T(8,128)S(1)}, f32[64,2,128]{2,0,1:T(8,128)S(1)}, u32[]{:S(2)}, u32[]{:S(2)}) collective-permute-start(f32[64,2,128]{2,0,1:T(8,128)S(1)} %get-tuple-element.92), channel_id=1, source_target_pairs={{4,0},{8,4},{12,8},{16,12},{20,16},{24,20},{28,24},{5,1},{9,5},{13... | collective-permute-start | bytes 196616 | tf_op jit(solution)/shard_map/ppermute | solution.py:25
  98.5 8.3 %collective-permute-start.9 = (f32[64,2,128]{2,0,1:T(8,128)S(1)}, f32[64,2,128]{2,0,1:T(8,128)S(1)}, u32[]{:S(2)}, u32[]{:S(2)}) collective-permute-start(f32[64,2,128]{2,0,1:T(8,128)S(1)} %get-tuple-element.93), channel_id=1, source_target_pairs={{0,4},{4,8},{8,12},{12,16},{16,20},{20,24},{24,28},{1,5},{5,9},{9,... | collective-permute-start | bytes 196616 | tf_op jit(solution)/shard_map/ppermute | solution.py:24
  112.7 22.6 %collective-permute-start.12 = (f32[64,68,2]{1,0,2:T(8,128)S(1)}, f32[64,68,2]{1,0,2:T(8,128)S(1)}, u32[]{:S(2)}, u32[]{:S(2)}) collective-permute-start(f32[64,68,2]{1,0,2:T(8,128)S(1)} %copy.120), channel_id=1, source_target_pairs={{1,0},{2,1},{3,2},{5,4},{6,5},{7,6},{9,8},{10,9},{11,10},{13,12},{... | collective-permute-start | bytes 104456 | tf_op jit(solution)/shard_map/ppermute | solution.py:25
  116.8 21.6 %collective-permute-start.13 = (f32[64,68,2]{1,0,2:T(8,128)S(1)}, f32[64,68,2]{1,0,2:T(8,128)S(1)}, u32[]{:S(2)}, u32[]{:S(2)}) collective-permute-start(f32[64,68,2]{1,0,2:T(8,128)S(1)} %copy.122), channel_id=1, source_target_pairs={{0,1},{1,2},{2,3},{4,5},{5,6},{6,7},{8,9},{9,10},{10,11},{12,13},{... | collective-permute-start | bytes 104456 | tf_op jit(solution)/shard_map/ppermute | solution.py:24
  128.5 39.1 %collective-permute-start.10 = (f32[64,2,128]{2,0,1:T(8,128)S(1)}, f32[64,2,128]{2,0,1:T(8,128)S(1)}, u32[]{:S(2)}, u32[]{:S(2)}) collective-permute-start(f32[64,2,128]{2,0,1:T(8,128)S(1)} %get-tuple-element.90), channel_id=1, source_target_pairs={{4,0},{8,4},{12,8},{16,12},{20,16},{24,20},{28,24},{5,1},{9,5},{13... | collective-permute-start | bytes 196616 | tf_op jit(solution)/shard_map/ppermute | solution.py:25
  129.8 37.8 %collective-permute-start.11 = (f32[64,2,128]{2,0,1:T(8,128)S(1)}, f32[64,2,128]{2,0,1:T(8,128)S(1)}, u32[]{:S(2)}, u32[]{:S(2)}) collective-permute-start(f32[64,2,128]{2,0,1:T(8,128)S(1)} %get-tuple-element.91), channel_id=1, source_target_pairs={{0,4},{4,8},{8,12},{12,16},{16,20},{20,24},{24,28},{1,5},{5,9},{9,... | collective-permute-start | bytes 196616 | tf_op jit(solution)/shard_map/ppermute | solution.py:24
  154.0 7.7 %collective-permute-start.14 = (f32[64,64,2]{1,0,2:T(8,128)S(1)}, f32[64,64,2]{1,0,2:T(8,128)S(1)}, u32[]{:S(2)}, u32[]{:S(2)}) collective-permute-start(f32[64,64,2]{1,0,2:T(8,128)S(1)} %copy.124), channel_id=1, source_target_pairs={{1,0},{2,1},{3,2},{5,4},{6,5},{7,6},{9,8},{10,9},{11,10},{13,12},{... | collective-permute-start | bytes 98312 | tf_op jit(solution)/shard_map/ppermute | solution.py:25
  157.9 6.7 %collective-permute-start.15 = (f32[64,64,2]{1,0,2:T(8,128)S(1)}, f32[64,64,2]{1,0,2:T(8,128)S(1)}, u32[]{:S(2)}, u32[]{:S(2)}) collective-permute-start(f32[64,64,2]{1,0,2:T(8,128)S(1)} %copy.126), channel_id=1, source_target_pairs={{0,1},{1,2},{2,3},{4,5},{5,6},{6,7},{8,9},{9,10},{10,11},{12,13},{... | collective-permute-start | bytes 98312 | tf_op jit(solution)/shard_map/ppermute | solution.py:24
  187.4 7.4 %collective-permute-start.16 = (f32[64,2,128]{2,0,1:T(8,128)S(1)}, f32[64,2,128]{2,0,1:T(8,128)S(1)}, u32[]{:S(2)}, u32[]{:S(2)}) collective-permute-start(f32[64,2,128]{2,0,1:T(8,128)S(1)} %get-tuple-element.84), channel_id=1, source_target_pairs={{4,0},{8,4},{12,8},{16,12},{20,16},{24,20},{28,24},{5,1},{9,5},{13... | collective-permute-start | bytes 196616 | tf_op jit(solution)/shard_map/ppermute | solution.py:25
  188.7 8.4 %collective-permute-start.17 = (f32[64,2,128]{2,0,1:T(8,128)S(1)}, f32[64,2,128]{2,0,1:T(8,128)S(1)}, u32[]{:S(2)}, u32[]{:S(2)}) collective-permute-start(f32[64,2,128]{2,0,1:T(8,128)S(1)} %get-tuple-element.85), channel_id=1, source_target_pairs={{0,4},{4,8},{8,12},{12,16},{16,20},{20,24},{24,28},{1,5},{5,9},{9,... | collective-permute-start | bytes 196616 | tf_op jit(solution)/shard_map/ppermute | solution.py:24
  202.0 10.1 %copy-start.3 = (f32[64,64,128]{2,0,1:T(8,128)S(1)}, f32[64,64,128]{2,0,1:T(8,128)}, u32[]{:S(2)}) copy-start(f32[64,64,128]{2,0,1:T(8,128)} %scatter-add.15) | copy-start | bytes 6291460
  205.0 20.6 %collective-permute-start.20 = (f32[64,68,2]{1,0,2:T(8,128)S(1)}, f32[64,68,2]{1,0,2:T(8,128)S(1)}, u32[]{:S(2)}, u32[]{:S(2)}) collective-permute-start(f32[64,68,2]{1,0,2:T(8,128)S(1)} %copy.129), channel_id=1, source_target_pairs={{1,0},{2,1},{3,2},{5,4},{6,5},{7,6},{9,8},{10,9},{11,10},{13,12},{... | collective-permute-start | bytes 104456 | tf_op jit(solution)/shard_map/ppermute | solution.py:25
  209.1 19.6 %collective-permute-start.21 = (f32[64,68,2]{1,0,2:T(8,128)S(1)}, f32[64,68,2]{1,0,2:T(8,128)S(1)}, u32[]{:S(2)}, u32[]{:S(2)}) collective-permute-start(f32[64,68,2]{1,0,2:T(8,128)S(1)} %copy.131), channel_id=1, source_target_pairs={{0,1},{1,2},{2,3},{4,5},{5,6},{6,7},{8,9},{9,10},{10,11},{12,13},{... | collective-permute-start | bytes 104456 | tf_op jit(solution)/shard_map/ppermute | solution.py:24
  219.0 39.2 %collective-permute-start.18 = (f32[64,2,128]{2,0,1:T(8,128)S(1)}, f32[64,2,128]{2,0,1:T(8,128)S(1)}, u32[]{:S(2)}, u32[]{:S(2)}) collective-permute-start(f32[64,2,128]{2,0,1:T(8,128)S(1)} %get-tuple-element.82), channel_id=1, source_target_pairs={{4,0},{8,4},{12,8},{16,12},{20,16},{24,20},{28,24},{5,1},{9,5},{13... | collective-permute-start | bytes 196616 | tf_op jit(solution)/shard_map/ppermute | solution.py:25
  220.3 37.9 %collective-permute-start.19 = (f32[64,2,128]{2,0,1:T(8,128)S(1)}, f32[64,2,128]{2,0,1:T(8,128)S(1)}, u32[]{:S(2)}, u32[]{:S(2)}) collective-permute-start(f32[64,2,128]{2,0,1:T(8,128)S(1)} %get-tuple-element.83), channel_id=1, source_target_pairs={{0,4},{4,8},{8,12},{12,16},{16,20},{20,24},{24,28},{1,5},{5,9},{9,... | collective-permute-start | bytes 196616 | tf_op jit(solution)/shard_map/ppermute | solution.py:24
  244.2 8.1 %collective-permute-start.22 = (f32[64,64,2]{1,0,2:T(8,128)S(1)}, f32[64,64,2]{1,0,2:T(8,128)S(1)}, u32[]{:S(2)}, u32[]{:S(2)}) collective-permute-start(f32[64,64,2]{1,0,2:T(8,128)S(1)} %copy.133), channel_id=1, source_target_pairs={{1,0},{2,1},{3,2},{5,4},{6,5},{7,6},{9,8},{10,9},{11,10},{13,12},{... | collective-permute-start | bytes 98312 | tf_op jit(solution)/shard_map/ppermute | solution.py:25
  248.1 7.1 %collective-permute-start.23 = (f32[64,64,2]{1,0,2:T(8,128)S(1)}, f32[64,64,2]{1,0,2:T(8,128)S(1)}, u32[]{:S(2)}, u32[]{:S(2)}) collective-permute-start(f32[64,64,2]{1,0,2:T(8,128)S(1)} %copy.135), channel_id=1, source_target_pairs={{0,1},{1,2},{2,3},{4,5},{5,6},{6,7},{8,9},{9,10},{10,11},{12,13},{... | collective-permute-start | bytes 98312 | tf_op jit(solution)/shard_map/ppermute | solution.py:24
  278.1 7.2 %collective-permute-start.24 = (f32[64,2,128]{2,0,1:T(8,128)S(1)}, f32[64,2,128]{2,0,1:T(8,128)S(1)}, u32[]{:S(2)}, u32[]{:S(2)}) collective-permute-start(f32[64,2,128]{2,0,1:T(8,128)S(1)} %get-tuple-element.76), channel_id=1, source_target_pairs={{4,0},{8,4},{12,8},{16,12},{20,16},{24,20},{28,24},{5,1},{9,5},{13... | collective-permute-start | bytes 196616 | tf_op jit(solution)/shard_map/ppermute | solution.py:25
  279.4 8.2 %collective-permute-start.25 = (f32[64,2,128]{2,0,1:T(8,128)S(1)}, f32[64,2,128]{2,0,1:T(8,128)S(1)}, u32[]{:S(2)}, u32[]{:S(2)}) collective-permute-start(f32[64,2,128]{2,0,1:T(8,128)S(1)} %get-tuple-element.77), channel_id=1, source_target_pairs={{0,4},{4,8},{8,12},{12,16},{16,20},{20,24},{24,28},{1,5},{5,9},{9,... | collective-permute-start | bytes 196616 | tf_op jit(solution)/shard_map/ppermute | solution.py:24
  292.4 10.1 %copy-start.5 = (f32[64,64,128]{2,0,1:T(8,128)S(1)}, f32[64,64,128]{2,0,1:T(8,128)}, u32[]{:S(2)}) copy-start(f32[64,64,128]{2,0,1:T(8,128)} %scatter-add.16) | copy-start | bytes 6291460
  295.4 20.8 %collective-permute-start.28 = (f32[64,68,2]{1,0,2:T(8,128)S(1)}, f32[64,68,2]{1,0,2:T(8,128)S(1)}, u32[]{:S(2)}, u32[]{:S(2)}) collective-permute-start(f32[64,68,2]{1,0,2:T(8,128)S(1)} %copy.138), channel_id=1, source_target_pairs={{1,0},{2,1},{3,2},{5,4},{6,5},{7,6},{9,8},{10,9},{11,10},{13,12},{... | collective-permute-start | bytes 104456 | tf_op jit(solution)/shard_map/ppermute | solution.py:25
  299.5 19.9 %collective-permute-start.29 = (f32[64,68,2]{1,0,2:T(8,128)S(1)}, f32[64,68,2]{1,0,2:T(8,128)S(1)}, u32[]{:S(2)}, u32[]{:S(2)}) collective-permute-start(f32[64,68,2]{1,0,2:T(8,128)S(1)} %copy.140), channel_id=1, source_target_pairs={{0,1},{1,2},{2,3},{4,5},{5,6},{6,7},{8,9},{9,10},{10,11},{12,13},{... | collective-permute-start | bytes 104456 | tf_op jit(solution)/shard_map/ppermute | solution.py:24
  309.4 39.6 %collective-permute-start.26 = (f32[64,2,128]{2,0,1:T(8,128)S(1)}, f32[64,2,128]{2,0,1:T(8,128)S(1)}, u32[]{:S(2)}, u32[]{:S(2)}) collective-permute-start(f32[64,2,128]{2,0,1:T(8,128)S(1)} %get-tuple-element.74), channel_id=1, source_target_pairs={{4,0},{8,4},{12,8},{16,12},{20,16},{24,20},{28,24},{5,1},{9,5},{13... | collective-permute-start | bytes 196616 | tf_op jit(solution)/shard_map/ppermute | solution.py:25
  310.7 38.3 %collective-permute-start.27 = (f32[64,2,128]{2,0,1:T(8,128)S(1)}, f32[64,2,128]{2,0,1:T(8,128)S(1)}, u32[]{:S(2)}, u32[]{:S(2)}) collective-permute-start(f32[64,2,128]{2,0,1:T(8,128)S(1)} %get-tuple-element.75), channel_id=1, source_target_pairs={{0,4},{4,8},{8,12},{12,16},{16,20},{20,24},{24,28},{1,5},{5,9},{9,... | collective-permute-start | bytes 196616 | tf_op jit(solution)/shard_map/ppermute | solution.py:24
  335.1 8.0 %collective-permute-start.30 = (f32[64,64,2]{1,0,2:T(8,128)S(1)}, f32[64,64,2]{1,0,2:T(8,128)S(1)}, u32[]{:S(2)}, u32[]{:S(2)}) collective-permute-start(f32[64,64,2]{1,0,2:T(8,128)S(1)} %copy.142), channel_id=1, source_target_pairs={{1,0},{2,1},{3,2},{5,4},{6,5},{7,6},{9,8},{10,9},{11,10},{13,12},{... | collective-permute-start | bytes 98312 | tf_op jit(solution)/shard_map/ppermute | solution.py:25
  339.0 7.1 %collective-permute-start.31 = (f32[64,64,2]{1,0,2:T(8,128)S(1)}, f32[64,64,2]{1,0,2:T(8,128)S(1)}, u32[]{:S(2)}, u32[]{:S(2)}) collective-permute-start(f32[64,64,2]{1,0,2:T(8,128)S(1)} %copy.144), channel_id=1, source_target_pairs={{0,1},{1,2},{2,3},{4,5},{5,6},{6,7},{8,9},{9,10},{10,11},{12,13},{... | collective-permute-start | bytes 98312 | tf_op jit(solution)/shard_map/ppermute | solution.py:24
  369.5 60.3 %copy-start.17 = (f32[64,64,128]{2,0,1:T(8,128)S(1)}, f32[64,64,128]{2,0,1:T(8,128)}, u32[]{:S(2)}) copy-start(f32[64,64,128]{2,0,1:T(8,128)} %scatter-add.19) | copy-start | bytes 6291460
  429.0 3.3 copy-start.1
  (11 other events, 21.3 us)
where the time goes:
time: 440 us; the launch traced here: 433 us
  local copies, waits for them, and re-layouts  140 us (32%)
  other arithmetic  133 us (30%)
  starting transfers between devices  99 us (22%)
  blocking collectives  43.3 us (10%)
  waiting for transfers between devices  8.04 us (2%)
  matrix products  6.69 us (2%)
    ppermute x16, starting transfers between devices, extended_2(): before = lax.ppermute(last, axis, up)  71.7 us
    add x4, other arithmetic, advance(): pressure - time_step * bulk * divergence  64 us
    slice x24, local copies, waits for them, and re-layouts, extended_2(): initial = lax.slice_in_dim(shard, 0, width, axis=dim)  48.1 us
    psum x1, blocking collectives, body(): total_gram = lax.psum(gram, ('strike', 'dip'))  43.3 us
    sub x4, other arithmetic, advance(): dip_vel = dip_vel - time_step * buoy * fourth_diff(extended[:, 2:-2, :], 2)  32.2 us
    ppermute x8, local copies, waits for them, and re-layouts, extended_2(): after = lax.ppermute(initial, axis, down)  24.4 us
    ppermute x8, local copies, waits for them, and re-layouts, extended_2(): before = lax.ppermute(last, axis, up)  24.2 us
    ppermute x16, starting transfers between devices, extended_2(): after = lax.ppermute(initial, axis, down)  20.6 us
  transfers between devices with their start and end apart: 34, of which 6 were waited for; matrix products, arithmetic and copies ran while one was open for 36% of the time, Pallas kernels for 0%

commit v1 on v0

v1 whole, which is shorter than its diff:
```python
import functools
import math

import jax
import jax.numpy as jnp
from jax import lax
from jax.experimental import pallas as pl
from jax.experimental.pallas import tpu as pltpu
from jax.sharding import PartitionSpec as P

MESH = pl.DeviceIdType.MESH
STEPS = 4
NCLASS = 8
TIME_STEP = 0.2
OFF = 16
CH = 16


def lane_diff(f):
    n = f.shape[-1]
    ax = f.ndim - 1
    near = pltpu.roll(f, n - 1, ax) - pltpu.roll(f, 1, ax)
    far = pltpu.roll(f, n - 2, ax) - pltpu.roll(f, 2, ax)
    return 8.0 * near - far


def kernel(
    ns,
    nd,
    scale,
    bulk_t,
    buoy_t,
    grav,
    classes,
    sens,
    p_hbm,
    sv_hbm,
    dv_hbm,
    k_hbm,
    out_p,
    out_g,
    pe,
    se,
    dv,
    vv,
    kv,
    kf,
    kt,
    bx,
    bk,
    bq,
    hb,
    inj,
    wrow,
    sp_lo,
    sp_hi,
    rp_lo,
    rp_hi,
    sq,
    rq_l,
    rq_r,
    ss_lo,
    ss_hi,
    rs_lo,
    rs_hi,
    sdq,
    rd_l,
    rd_r,
    rb_lo,
    rb_hi,
    rbq_l,
    rbq_r,
    hv,
    qv,
    edge_a,
    edge_b,
    sens_all,
    gram,
    part1,
    part2,
    in_sem,
    out_sem,
    halo_s,
    halo_r,
    vel_s,
    vel_r,
    buo_s,
    buo_r,
    sens_s,
    sens_r,
    red1_s,
    red1_r,
    red2_s,
    red2_r,
    red3_s,
    red3_r,
):
    levels = p_hbm.shape[0]
    rows = p_hbm.shape[1]
    nch = levels // CH
    probes = k_hbm.shape[0]
    si = lax.axis_index("strike")
    di = lax.axis_index("dip")
    END = OFF + rows

    def strike_peer(o):
        return (lax.rem(si + o, ns), di)

    def dip_peer(o):
        return (si, lax.rem(di + o, nd))

    has = (si > 0, si < ns - 1, di > 0, di < nd - 1)
    peer = ((si - 1, di), (si + 1, di), (si, di - 1), (si, di + 1))

    in_p = pltpu.make_async_copy(p_hbm, pe.at[pl.ds(1, levels), pl.ds(OFF, rows), :], in_sem.at[0])
    in_s = pltpu.make_async_copy(sv_hbm, se.at[:, pl.ds(OFF, rows), :], in_sem.at[1])
    in_d = pltpu.make_async_copy(dv_hbm, dv, in_sem.at[2])
    in_k = pltpu.make_async_copy(k_hbm, kv, in_sem.at[3])
    in_p.start()
    in_s.start()
    in_d.start()
    in_k.start()

    barrier = pltpu.get_barrier_semaphore()
    for o in range(1, ns):
        pl.semaphore_signal(barrier, inc=1, device_id=strike_peer(o), device_id_type=MESH)
    for o in range(1, nd):
        pl.semaphore_signal(barrier, inc=1, device_id=dip_peer(o), device_id_type=MESH)

    lane = lax.broadcasted_iota(jnp.int32, (rows, 128), 1)
    slot = lane // 8
    low = (lane % 8) < 4
    rim = (lane < 2) | (lane >= 126)

    cls = classes[...]
    buoy = jnp.zeros((rows, 128), jnp.float32)
    bulk = jnp.zeros((rows, 128), jnp.float32)
    for i in range(NCLASS):
        buoy = jnp.where(cls == i, buoy_t[i], buoy)
        bulk = jnp.where(cls == i, bulk_t[i], bulk)
    bk[...] = bulk * (TIME_STEP / 12.0)
    bx[pl.ds(OFF, rows), :] = buoy * (TIME_STEP / 12.0)
    first = jnp.where(lane < 8, pltpu.roll(buoy * (TIME_STEP / 12.0), 4, 1), 0.0)
    for width in (8, 16, 32, 64):
        first = first + pltpu.roll(first, width, 1)
    bq[...] = first

    zero_block = jnp.zeros((rows, 128), jnp.float32)
    pe[0, pl.ds(OFF, rows), :] = zero_block
    pe[levels + 1, pl.ds(OFF, rows), :] = zero_block
    vv[0] = zero_block
    vv[levels + 1] = zero_block

    def zero_when(cond, *refs):
        @pl.when(jnp.logical_not(cond))
        def _():
            for r in refs:
                r[...] = jnp.zeros(r.shape, r.dtype)

    zero_when(has[0], rp_lo, rs_lo, rb_lo)
    zero_when(has[1], rp_hi, rs_hi, rb_hi)
    zero_when(has[2], rq_l, rd_l, rbq_l)
    zero_when(has[3], rq_r, rd_r, rbq_r)

    pl.semaphore_wait(barrier, ns - 1 + nd - 1)

    def remote(src, dst, s, r, to):
        return pltpu.make_async_remote_copy(
            src_ref=src, dst_ref=dst, send_sem=s, recv_sem=r, device_id=to, device_id_type=MESH
        )

    def halo_copy(k, c, i):
        src = (sp_lo, sp_hi, sq, sq)[i].at[k, c]
        dst = (rp_hi, rp_lo, rq_r, rq_l)[i].at[k, c]
        return remote(src, dst, halo_s.at[k, c, i], halo_r.at[k, c, i], peer[i])

    def vel_copy(c, i):
        src = (ss_lo, ss_hi, sdq, sdq)[i].at[c]
        dst = (rs_hi, rs_lo, rd_r, rd_l)[i].at[c]
        return remote(src, dst, vel_s.at[c, i], vel_r.at[c, i], peer[i])

    def buo_copy(i):
        src = (bx.at[pl.ds(OFF, 8), :], bx.at[pl.ds(END - 8, 8), :], bq, bq)[i]
        dst = (rb_hi, rb_lo, rbq_r, rbq_l)[i]
        return remote(src, dst, buo_s.at[i], buo_r.at[i], peer[i])

    def each_side(make, what):
        for i in range(4):
            cond = has[i ^ 1] if what == "recv" else has[i]

            @pl.when(cond)
            def _(i=i):
                copy = make(i)
                if what == "start":
                    copy.start()
                elif what == "recv":
                    copy.wait_recv()
                else:
                    copy.wait_send()

    def sens_copy(o):
        return remote(sens, sens_all.at[di], sens_s.at[o - 1], sens_r.at[o - 1], dip_peer(o))

    each_side(buo_copy, "start")
    for o in range(1, nd):
        sens_copy(o).start()

    zero_pack = jnp.zeros((rows, 128), jnp.float32)

    def packed(acc, field, j):
        return jnp.where(slot == j, pltpu.roll(field, 8 * j + 4, 1), acc)

    in_p.wait()
    in_s.wait()
    in_d.wait()

    for c in reversed(range(nch)):

        def pack_first(j, accs, c=c):
            lev = c * CH + j
            f = pe[lev + 1, pl.ds(OFF, rows), :]
            sp_lo[0, c, j] = f[0:4]
            sp_hi[0, c, j] = f[rows - 4 : rows]
            ss_lo[c, j] = se[lev, pl.ds(OFF, 8), :][0:2]
            ss_hi[c, j] = se[lev, pl.ds(END - 8, 8), :][6:8]
            return packed(accs[0], f, j), packed(accs[1], dv[lev], j)

        a, b = lax.fori_loop(0, CH, pack_first, (zero_pack, zero_pack))
        sq[0, c] = a
        sdq[c] = b
        each_side(lambda i, c=c: halo_copy(0, c, i), "start")
        each_side(lambda i, c=c: vel_copy(c, i), "start")

    in_k.wait()

    def widen(i, _):
        kf[pl.ds(pl.multiple_of(i * rows, rows), rows), :] = kv[i].astype(jnp.float32)
        return 0

    lax.fori_loop(0, probes, widen, 0)
    half = rows // 2

    def regroup(x, _):
        kt[x, :, 0:128] = kf[pl.ds(x, probes, stride=rows), :].astype(jnp.bfloat16)
        kt[x, :, 128:256] = kf[pl.ds(x + half, probes, stride=rows), :].astype(jnp.bfloat16)
        return 0

    lax.fori_loop(0, half, regroup, 0)

    sens_all[di] = sens[...]
    for o in range(1, nd):
        sens_copy(o).wait_recv()
    every = sens_all[...].reshape(nd * 8, 128)
    mine = every[:, 5:6] == di.astype(jnp.float32)
    cell = every[:, 4:5].astype(jnp.int32)
    slane = lax.broadcasted_iota(jnp.int32, (nd * 8, 128), 1)
    at_row = (lax.shift_right_logical(cell, 7) == slane) & mine
    at_col = ((cell & 127) == slane).astype(jnp.float32)
    for k in range(STEPS):
        left = jnp.where(at_row, every[:, k : k + 1], 0.0)
        placed = lax.dot_general(
            left,
            at_col,
            (((0,), (0,)), ((), ())),
            precision=lax.Precision.HIGHEST,
            preferred_element_type=jnp.float32,
        )
        inj[k] = placed[0:rows]

    each_side(buo_copy, "recv")
    bx[pl.ds(OFF - 8, 8), :] = rb_lo[...]
    bx[pl.ds(END, 8), :] = rb_hi[...]
    hb[...] = jnp.where(low, rbq_l[...], rbq_r[...])

    def phase_a(k, c):
        each_side(lambda i: halo_copy(k, c, i), "recv")
        if k == 0:
            each_side(lambda i: vel_copy(c, i), "recv")
            hv[c] = jnp.where(low, rd_l[c], rd_r[c])
        own = sq[k, c]
        d_left = lane_diff(jnp.where(low, rq_l[k, c], own))
        d_right = lane_diff(jnp.where(low, own, rq_r[k, c]))
        hv[c] = hv[c] - hb[...] * jnp.where(low, d_left, d_right)
        edge_a[...] = jnp.where(low, d_right, d_left)

        def level(j, acc):
            lev = c * CH + j
            pe[lev + 1, pl.ds(OFF - 4, 4), :] = rp_lo[k, c, j]
            pe[lev + 1, pl.ds(END, 4), :] = rp_hi[k, c, j]
            if k == 0:
                se[lev, pl.ds(OFF - 2, 2), :] = rs_lo[c, j]
                se[lev, pl.ds(END, 2), :] = rs_hi[c, j]

            def win(o):
                return pe[lev + 1, pl.ds(OFF - 8 + o, rows + 16), :]

            ds = 8.0 * (win(1) - win(-1)) - (win(2) - win(-2))
            ext = pl.ds(OFF - 8, rows + 16)
            se[lev, ext, :] = se[lev, ext, :] - bx[ext, :] * ds
            own_rows = pl.ds(OFF, rows)
            b = bx[own_rows, :]
            dd = jnp.where(rim, pltpu.roll(edge_a[...], 124 - 8 * j, 1), lane_diff(pe[lev + 1, own_rows, :]))
            v = dv[lev] - b * dd
            dv[lev] = v
            dz = (6.0 * b) * (pe[lev + 2, own_rows, :] - pe[lev, own_rows, :])
            vv[lev + 1] = -dz if k == 0 else vv[lev + 1] - dz
            return packed(acc, v, j)

        qv[c] = lax.fori_loop(0, CH, level, zero_pack)

    def phase_b(k, c):
        last = k == STEPS - 1
        own = qv[c]
        halo = hv[c]
        d_left = lane_diff(jnp.where(low, halo, own))
        d_right = lane_diff(jnp.where(low, own, halo))
        edge_b[...] = jnp.where(low, d_right, d_left)

        def level(j, acc):
            lev = c * CH + j

            def win(o):
                return se[lev, pl.ds(OFF + o, rows), :]

            ds = 8.0 * (win(1) - win(-1)) - (win(2) - win(-2))
            dd = jnp.where(rim, pltpu.roll(edge_b[...], 124 - 8 * j, 1), lane_diff(dv[lev]))
            dz = 6.0 * (vv[lev + 2] - vv[lev])
            own_rows = pl.ds(OFF, rows)
            f = pe[lev + 1, own_rows, :] - bk[...] * (ds + dd + dz) + (TIME_STEP * grav[lev]) * vv[lev + 1]
            if c == nch - 1:
                f = f + jnp.where(j == CH - 1, inj[k], 0.0)
            pe[lev + 1, own_rows, :] = f
            if last:
                return acc
            sp_lo[k + 1, c, j] = f[0:4]
            sp_hi[k + 1, c, j] = f[rows - 4 : rows]
            return packed(acc, f, j)

        acc = lax.fori_loop(0, CH, level, zero_pack)
        if not last:
            sq[k + 1, c] = acc
            each_side(lambda i: halo_copy(k + 1, c, i), "start")
        else:
            out_copy(c).start()

    def out_copy(c):
        return pltpu.make_async_copy(
            pe.at[pl.ds(1 + c * CH, CH), pl.ds(OFF, rows), :], out_p.at[pl.ds(c * CH, CH)], out_sem.at[c]
        )

    share = gram.shape[1]

    def red1(o):
        to = lax.rem(di + o, nd)
        return remote(gram.at[to], part1.at[o - 1], red1_s.at[o - 1], red1_r.at[o - 1], dip_peer(o))

    def red2(o):
        return remote(part2.at[si], part2.at[si], red2_s.at[o - 1], red2_r.at[o - 1], strike_peer(o))

    def red3(o):
        return remote(out_g.at[di], out_g.at[di], red3_s.at[o - 1], red3_r.at[o - 1], dip_peer(o))

    def reduce_start():
        sea = pe[levels, pl.ds(OFF, rows), :] * scale
        wrow[...] = sea * sea

        def body(x, acc):
            kx = kt[x]
            w = jnp.concatenate([wrow[pl.ds(x, 1), :], wrow[pl.ds(x + half, 1), :]], axis=1)
            kw = kx.astype(jnp.float32) * w
            hi = kw.astype(jnp.bfloat16)
            lo = (kw - hi.astype(jnp.float32)).astype(jnp.bfloat16)
            both = jnp.concatenate([hi, lo], axis=0)
            return acc + lax.dot_general(
                both, kx, (((1,), (1,)), ((), ())), preferred_element_type=jnp.float32
            )

        acc = lax.fori_loop(0, half, body, jnp.zeros((2 * probes, probes), jnp.float32))
        total = acc[0:probes] + acc[probes : 2 * probes]
        total = jnp.concatenate([total, jnp.zeros((probes, 128 - probes), jnp.float32)], axis=1)
        if nd * share > probes:
            total = jnp.concatenate([total, jnp.zeros((nd * share - probes, 128), jnp.float32)], axis=0)
        for d in range(nd):
            gram[d] = total[d * share : (d + 1) * share]
        for o in range(1, nd):
            red1(o).start()

    def reduce_middle():
        s = gram[di]
        for o in range(1, nd):
            red1(o).wait_recv()
            s = s + part1[o - 1]
        part2[si] = s
        for o in range(1, ns):
            red2(o).start()

    def reduce_spread():
        for o in range(1, ns):
            red2(o).wait_recv()
        s = part2[0]
        for i in range(1, ns):
            s = s + part2[i]
        out_g[di] = s
        for o in range(1, nd):
            red3(o).start()

    stages = [reduce_start, reduce_middle, reduce_spread]
    for k in range(STEPS):
        phase_a(k, nch - 1)
        for c in reversed(range(nch)):
            if c > 0:
                phase_a(k, c - 1)
            phase_b(k, c)
            if k == STEPS - 1 and stages:
                stages.pop(0)()
    for stage in stages:
        stage()

    for c in range(nch):
        out_copy(c).wait()
        each_side(lambda i, c=c: vel_copy(c, i), "send")
        for k in range(STEPS):
            each_side(lambda i, c=c, k=k: halo_copy(k, c, i), "send")
    each_side(buo_copy, "send")
    for o in range(1, nd):
        sens_copy(o).wait_send()
        red1(o).wait_send()
        red3(o).wait_recv()
        red3(o).wait_send()
    for o in range(1, ns):
        red2(o).wait_send()


def body(
    ns,
    nd,
    pressure,
    strike_vel,
    dip_vel,
    bathy_class,
    bulk_table,
    buoy_table,
    gravity,
    sensor_amp,
    sensor_owner,
    sensor_cell,
    probe_kernel,
):
    levels, rows, cols = pressure.shape
    probes = probe_kernel.shape[0]
    nch = levels // CH
    share = -(-probes // (8 * nd)) * 8
    scale = 1.0 / math.sqrt(rows * cols * ns * nd)
    sens = jnp.concatenate(
        [
            sensor_amp.T,
            sensor_cell.astype(jnp.float32)[:, None],
            sensor_owner.astype(jnp.float32),
            jnp.zeros((sensor_amp.shape[1], 128 - STEPS - 2), jnp.float32),
        ],
        axis=1,
    )
    f32 = jnp.float32

    def vmem(*shape, dtype=f32):
        return pltpu.VMEM(shape, dtype)

    def sems(*shape):
        return pltpu.SemaphoreType.DMA(shape)

    scratch = [
        vmem(levels + 2, rows + 2 * OFF, cols),
        vmem(levels, rows + 2 * OFF, cols),
        vmem(levels, rows, cols),
        vmem(levels + 2, rows, cols),
        vmem(probes, rows, cols, dtype=jnp.bfloat16),
        vmem(probes * rows, cols),
        vmem(rows // 2, probes, 2 * cols, dtype=jnp.bfloat16),
        vmem(rows + 2 * OFF, cols),
        vmem(rows, cols),
        vmem(rows, cols),
        vmem(rows, cols),
        vmem(STEPS, rows, cols),
        vmem(rows, cols),
        vmem(STEPS, nch, CH, 4, cols),
        vmem(STEPS, nch, CH, 4, cols),
        vmem(STEPS, nch, CH, 4, cols),
        vmem(STEPS, nch, CH, 4, cols),
        vmem(STEPS, nch, rows, cols),
        vmem(STEPS, nch, rows, cols),
        vmem(STEPS, nch, rows, cols),
        vmem(nch, CH, 2, cols),
        vmem(nch, CH, 2, cols),
        vmem(nch, CH, 2, cols),
        vmem(nch, CH, 2, cols),
        vmem(nch, rows, cols),
        vmem(nch, rows, cols),
        vmem(nch, rows, cols),
        vmem(8, cols),
        vmem(8, cols),
        vmem(rows, cols),
        vmem(rows, cols),
        vmem(nch, rows, cols),
        vmem(nch, rows, cols),
        vmem(rows, cols),
        vmem(rows, cols),
        vmem(nd, 8, cols),
        vmem(nd, share, cols),
        vmem(nd - 1, share, cols),
        vmem(ns, share, cols),
        sems(4),
        sems(nch),
        sems(STEPS, nch, 4),
        sems(STEPS, nch, 4),
        sems(nch, 4),
        sems(nch, 4),
        sems(4),
        sems(4),
        sems(nd - 1),
        sems(nd - 1),
        sems(nd - 1),
        sems(nd - 1),
        sems(ns - 1),
        sems(ns - 1),
        sems(nd - 1),
        sems(nd - 1),
    ]
    smem = pl.BlockSpec(memory_space=pltpu.SMEM)
    whole = pl.BlockSpec(memory_space=pltpu.VMEM)
    hbm = pl.BlockSpec(memory_space=pl.ANY)
    final, gram = pl.pallas_call(
        functools.partial(kernel, ns, nd, scale),
        out_shape=(
            jax.ShapeDtypeStruct(pressure.shape, f32),
            jax.ShapeDtypeStruct((nd, share, cols), f32),
        ),
        in_specs=[smem, smem, smem, whole, whole, hbm, hbm, hbm, hbm],
        out_specs=(hbm, whole),
        scratch_shapes=scratch,
        compiler_params=pltpu.CompilerParams(
            collective_id=0, has_side_effects=True, vmem_limit_bytes=48 * 2**20
        ),
    )(bulk_table, buoy_table, gravity, bathy_class, sens, pressure, strike_vel, dip_vel, probe_kernel)
    gram = gram.reshape(nd * share, cols)[:probes, :probes]
    return final, jnp.linalg.cholesky(gram).T


def solution(mesh):
    return jax.shard_map(
        functools.partial(body, mesh.shape["strike"], mesh.shape["dip"]),
        mesh=mesh,
        in_specs=(
            P(None, "strike", "dip"),
            P(None, "strike", "dip"),
            P(None, "strike", "dip"),
            P("strike", "dip"),
            P(),
            P(),
            P(),
            P(None, ("strike", "dip")),
            P(("strike", "dip"), None),
            P(("strike", "dip")),
            P(None, "strike", "dip"),
        ),
        out_specs=(P(None, "strike", "dip"), P()),
        check_vma=False,
    )
```

time: 440 us -> 144 us (0.33); the launches traced: 433 us -> 144 us
  local copies, waits for them, and re-layouts: 140 us -> 8.83 us
  Pallas kernels: 0 us -> 123 us
  other arithmetic: 133 us -> 11.5 us
  starting transfers between devices: 99 us -> 0 us
  blocking collectives: 43.3 us -> 0 us
  waiting for transfers between devices: 8.04 us -> 0 us
  matrix products: 6.69 us -> 0 us
    pallas_call x0 -> x1, Pallas kernels: none -> 123 us  [body(): pl.pallas_call(functools.partial(kernel, ns, nd, scale), out_shape=(jax.S...]
    ppermute x32 -> x0, starting transfers between devices: 92.3 us -> none  [the longest x16 71.7 us: extended_2(): before = lax.ppermute(last, axis, up)]
    slice x32 -> x0, local copies, waits for them, and re-layouts: 68.5 us -> none  [the longest x24 48.1 us: extended_2(): initial = lax.slice_in_dim(shard, 0, width, axis=dim)]
    add x8 -> x0, other arithmetic: 64.2 us -> none  [the longest x4 64 us: advance(): pressure - time_step * bulk * divergence]
    sub x8 -> x0, other arithmetic: 52.4 us -> none  [the longest x4 32.2 us: advance(): dip_vel = dip_vel - time_step * buoy * fourth_diff(extended[:, 2:-2, :], 2)]
    ppermute x16 -> x0, local copies, waits for them, and re-layouts: 48.5 us -> none  [the longest x8 24.4 us: extended_2(): after = lax.ppermute(initial, axis, down)]
    psum x1 -> x0, blocking collectives: 43.3 us -> none  [body(): total_gram = lax.psum(gram, ('strike', 'dip'))]
    ppermute x32 -> x0, waiting for transfers between devices: 8.04 us -> none  [the longest x16 6.81 us: extended_2(): before = lax.ppermute(last, axis, up)]
  transfers between devices with their start and end apart: 34 -> 0, of which waited for: 6 -> 0; matrix products, arithmetic and copies ran while one was open for 36% -> 0% of each run, Pallas kernels for 0% -> 0%
where the time goes in v1:
time: 144 us
  Pallas kernels  123 us (85%)
  other arithmetic  11.5 us (8%)
  local copies, waits for them, and re-layouts  8.83 us (6%)
    pallas_call x1, Pallas kernels, body(): pl.pallas_call(functools.partial(kernel, ns, nd, scale), out_shape=(jax.S...  123 us
    another operation x3, other arithmetic, body(): return (final, jnp.linalg.cholesky(gram).T)  9.45 us
    unnamed x16, local copies, waits for them, and re-layouts  8.59 us

profile of v1, /device:TPU:0, one launch (start us, length us, event | category | flops | bytes accessed | tf_op | source)
XLA Modules:
  0.0 143.7 jit_solution(16932984134966028654)
XLA Ops:
  0.6 0.7 convert_element_type.7
  1.3 0.7 convert_bitcast_fusion
  1.9 0.1 pad.3.clone
  2.0 0.1 copy.20
  2.1 0.1 copy.21
  2.2 0.8 copy.19
  2.9 0.1 maximum_maximum_fusion.sens
  3.0 0.0 copy-start
  3.0 1.6 %copy-done = f32[64,64,128]{2,1,0:T(8,128)S(1)} copy-done((f32[64,64,128]{2,1,0:T(8,128)S(1)}, f32[64,64,128]{2,1,0:T(8,128)}, u32[]{:S(2)}) %copy-start) | copy-done | bytes 2097176
  4.6 0.0 copy-start.1
  4.6 1.4 copy-done.1
  6.0 0.0 copy-start.2
  6.0 0.8 copy-done.2
  6.8 0.0 copy-start.3
  6.8 0.7 copy-done.3
  7.4 0.0 copy-start.4
  7.4 0.7 copy-done.4
  8.1 0.0 copy-start.5
  8.1 0.7 copy-done.5
  8.7 122.7 %shard_map.122 = (f32[64,64,128]{2,1,0:T(8,128)S(1)}, f32[4,24,128]{2,1,0:T(8,128)S(1)}) custom-call(f32[8]{0:T(128)S(1)} %copy-done.3, f32[8]{0:T(128)S(1)} %copy-done.4, f32[64]{0:T(128)S(1)} %copy-done.5, s32[64,128]{1,0:T(8,128)S(1)} %copy-done.2, f32[8,128]{1,0:T(8,128)S(1)} %maximum_maximum_fusion.sens, f32[64,64,128]{2,1,0:T(8,128)S(1)} %copy-done, ...), custom_call_target="tpu_custom_call" | custom-call | tf_op jit(solution)/shard_map/pallas_call | solution.py:531
  131.4 0.1 copy.25
  131.5 8.8 %cholesky.18 = f32[96,96]{1,0:T(8,128)S(1)} custom-call(f32[96,96]{1,0:T(8,128)S(1)} %fusion), custom_call_target="Cholesky" | custom-call | tf_op jit(solution)/shard_map/jit(cholesky)/cholesky | solution.py:545
  140.3 0.6 compare_reduce_fusion
  141.0 0.7 select_bitcast_fusion
  141.6 0.7 copy.24
  142.4 1.3 copy.27
  (3 shorter events, 0.0 us)
Async XLA Ops:
  3.0 1.6 %copy-start = (f32[64,64,128]{2,1,0:T(8,128)S(1)}, f32[64,64,128]{2,1,0:T(8,128)}, u32[]{:S(2)}) copy-start(f32[64,64,128]{2,1,0:T(8,128)} %p_hbm.1) | copy-start | bytes 6291460
  4.6 1.4 copy-start.1
  6.0 0.8 copy-start.2
  6.8 0.7 copy-start.3
  7.4 0.7 copy-start.4
  8.1 0.7 copy-start.5

commit v2 on v1

--- a/solution.py
+++ b/solution.py
@@ -148,8 +148,12 @@
     zero_block = jnp.zeros((rows, 128), jnp.float32)
     pe[0, pl.ds(OFF, rows), :] = zero_block
     pe[levels + 1, pl.ds(OFF, rows), :] = zero_block
-    vv[0] = zero_block
-    vv[levels + 1] = zero_block
+
+    def clear(i, _):
+        vv[i] = zero_block
+        return 0
+
+    lax.fori_loop(0, levels + 2, clear, 0)
 
     def zero_when(cond, *refs):
         @pl.when(jnp.logical_not(cond))
@@ -225,7 +229,7 @@
             ss_hi[c, j] = se[lev, pl.ds(END - 8, 8), :][6:8]
             return packed(accs[0], f, j), packed(accs[1], dv[lev], j)
 
-        a, b = lax.fori_loop(0, CH, pack_first, (zero_pack, zero_pack))
+        a, b = lax.fori_loop(0, CH, pack_first, (zero_pack, zero_pack), unroll=8)
         sq[0, c] = a
         sdq[c] = b
         each_side(lambda i, c=c: halo_copy(0, c, i), "start")
@@ -237,7 +241,7 @@
         kf[pl.ds(pl.multiple_of(i * rows, rows), rows), :] = kv[i].astype(jnp.float32)
         return 0
 
-    lax.fori_loop(0, probes, widen, 0)
+    lax.fori_loop(0, probes, widen, 0, unroll=8)
     half = rows // 2
 
     def regroup(x, _):
@@ -245,7 +249,7 @@
         kt[x, :, 128:256] = kf[pl.ds(x + half, probes, stride=rows), :].astype(jnp.bfloat16)
         return 0
 
-    lax.fori_loop(0, half, regroup, 0)
+    lax.fori_loop(0, half, regroup, 0, unroll=4)
 
     sens_all[di] = sens[...]
     for o in range(1, nd):
@@ -274,9 +278,17 @@
 
     def phase_a(k, c):
         each_side(lambda i: halo_copy(k, c, i), "recv")
-        if k == 0:
+        base = c * CH
+
+        @pl.when(k == 0)
+        def _():
             each_side(lambda i: vel_copy(c, i), "recv")
             hv[c] = jnp.where(low, rd_l[c], rd_r[c])
+            se[pl.ds(base, CH), pl.ds(OFF - 2, 2), :] = rs_lo[c]
+            se[pl.ds(base, CH), pl.ds(END, 2), :] = rs_hi[c]
+
+        pe[pl.ds(base + 1, CH), pl.ds(OFF - 4, 4), :] = rp_lo[k, c]
+        pe[pl.ds(base + 1, CH), pl.ds(END, 4), :] = rp_hi[k, c]
         own = sq[k, c]
         d_left = lane_diff(jnp.where(low, rq_l[k, c], own))
         d_right = lane_diff(jnp.where(low, own, rq_r[k, c]))
@@ -284,12 +296,7 @@
         edge_a[...] = jnp.where(low, d_right, d_left)
 
         def level(j, acc):
-            lev = c * CH + j
-            pe[lev + 1, pl.ds(OFF - 4, 4), :] = rp_lo[k, c, j]
-            pe[lev + 1, pl.ds(END, 4), :] = rp_hi[k, c, j]
-            if k == 0:
-                se[lev, pl.ds(OFF - 2, 2), :] = rs_lo[c, j]
-                se[lev, pl.ds(END, 2), :] = rs_hi[c, j]
+            lev = base + j
 
             def win(o):
                 return pe[lev + 1, pl.ds(OFF - 8 + o, rows + 16), :]
@@ -303,13 +310,16 @@
             v = dv[lev] - b * dd
             dv[lev] = v
             dz = (6.0 * b) * (pe[lev + 2, own_rows, :] - pe[lev, own_rows, :])
-            vv[lev + 1] = -dz if k == 0 else vv[lev + 1] - dz
+            vv[lev + 1] = vv[lev + 1] - dz
             return packed(acc, v, j)
 
-        qv[c] = lax.fori_loop(0, CH, level, zero_pack)
+        acc = zero_pack
+        for j in range(CH):
+            acc = level(j, acc)
+        qv[c] = acc
 
     def phase_b(k, c):
-        last = k == STEPS - 1
+        base = c * CH
         own = qv[c]
         halo = hv[c]
         d_left = lane_diff(jnp.where(low, halo, own))
@@ -317,7 +327,7 @@
         edge_b[...] = jnp.where(low, d_right, d_left)
 
         def level(j, acc):
-            lev = c * CH + j
+            lev = base + j
 
             def win(o):
                 return se[lev, pl.ds(OFF + o, rows), :]
@@ -327,20 +337,24 @@
             dz = 6.0 * (vv[lev + 2] - vv[lev])
             own_rows = pl.ds(OFF, rows)
             f = pe[lev + 1, own_rows, :] - bk[...] * (ds + dd + dz) + (TIME_STEP * grav[lev]) * vv[lev + 1]
-            if c == nch - 1:
-                f = f + jnp.where(j == CH - 1, inj[k], 0.0)
+            if j == CH - 1:
+                f = f + jnp.where(c == nch - 1, inj[k], 0.0)
             pe[lev + 1, own_rows, :] = f
-            if last:
-                return acc
             sp_lo[k + 1, c, j] = f[0:4]
             sp_hi[k + 1, c, j] = f[rows - 4 : rows]
             return packed(acc, f, j)
 
-        acc = lax.fori_loop(0, CH, level, zero_pack)
-        if not last:
-            sq[k + 1, c] = acc
+        acc = zero_pack
+        for j in range(CH):
+            acc = level(j, acc)
+        sq[k + 1, c] = acc
+
+        @pl.when(k < STEPS - 1)
+        def _():
             each_side(lambda i: halo_copy(k + 1, c, i), "start")
-        else:
+
+        @pl.when(k == STEPS - 1)
+        def _():
             out_copy(c).start()
 
     def out_copy(c):
@@ -375,7 +389,7 @@
                 both, kx, (((1,), (1,)), ((), ())), preferred_element_type=jnp.float32
             )
 
-        acc = lax.fori_loop(0, half, body, jnp.zeros((2 * probes, probes), jnp.float32))
+        acc = lax.fori_loop(0, half, body, jnp.zeros((2 * probes, probes), jnp.float32), unroll=8)
         total = acc[0:probes] + acc[probes : 2 * probes]
         total = jnp.concatenate([total, jnp.zeros((probes, 128 - probes), jnp.float32)], axis=1)
         if nd * share > probes:
@@ -404,17 +418,27 @@
         for o in range(1, nd):
             red3(o).start()
 
-    stages = [reduce_start, reduce_middle, reduce_spread]
-    for k in range(STEPS):
-        phase_a(k, nch - 1)
-        for c in reversed(range(nch)):
-            if c > 0:
-                phase_a(k, c - 1)
-            phase_b(k, c)
-            if k == STEPS - 1 and stages:
-                stages.pop(0)()
-    for stage in stages:
-        stage()
+    def turn(t, _):
+        k = t // (nch + 1)
+        i = t % (nch + 1)
+
+        @pl.when(i < nch)
+        def _():
+            phase_a(k, nch - 1 - i)
+
+        @pl.when(i > 0)
+        def _():
+            phase_b(k, nch - i)
+
+        for at, stage in ((1, reduce_start), (2, reduce_middle), (3, reduce_spread)):
+
+            @pl.when((k == STEPS - 1) & (i == at))
+            def _(stage=stage):
+                stage()
+
+        return 0
+
+    lax.fori_loop(0, STEPS * (nch + 1), turn, 0)
 
     for c in range(nch):
         out_copy(c).wait()
@@ -482,11 +506,11 @@
         vmem(rows, cols),
         vmem(STEPS, rows, cols),
         vmem(rows, cols),
+        vmem(STEPS + 1, nch, CH, 4, cols),
+        vmem(STEPS + 1, nch, CH, 4, cols),
         vmem(STEPS, nch, CH, 4, cols),
         vmem(STEPS, nch, CH, 4, cols),
-        vmem(STEPS, nch, CH, 4, cols),
-        vmem(STEPS, nch, CH, 4, cols),
-        vmem(STEPS, nch, rows, cols),
+        vmem(STEPS + 1, nch, rows, cols),
         vmem(STEPS, nch, rows, cols),
         vmem(STEPS, nch, rows, cols),
         vmem(nch, CH, 2, cols),
@@ -538,7 +562,7 @@
         out_specs=(hbm, whole),
         scratch_shapes=scratch,
         compiler_params=pltpu.CompilerParams(
-            collective_id=0, has_side_effects=True, vmem_limit_bytes=48 * 2**20
+            collective_id=0, has_side_effects=True, vmem_limit_bytes=60 * 2**20
         ),
     )(bulk_table, buoy_table, gravity, bathy_class, sens, pressure, strike_vel, dip_vel, probe_kernel)
     gram = gram.reshape(nd * share, cols)[:probes, :probes]

time: 144 us -> 105 us (0.73)
  Pallas kernels: 123 us -> 85.6 us
  local copies, waits for them, and re-layouts: 8.83 us -> 5.74 us
    pallas_call x1, Pallas kernels: 123 us -> 85.6 us  [body(): pl.pallas_call(functools.partial(kernel, ns, nd, scale), out_shape=(jax.S...]
    unnamed x16 -> x4, local copies, waits for them, and re-layouts: 8.59 us -> 5.5 us
where the time goes in v2:
time: 105 us
  Pallas kernels  85.6 us (82%)
  other arithmetic  12.9 us (12%)
  local copies, waits for them, and re-layouts  5.74 us (5%)
    pallas_call x1, Pallas kernels, body(): pl.pallas_call(functools.partial(kernel, ns, nd, scale), out_shape=(jax.S...  85.6 us
    another operation x3, other arithmetic, body(): return (final, jnp.linalg.cholesky(gram).T)  9.45 us
    unnamed x4, local copies, waits for them, and re-layouts  5.5 us

profile of v2, /device:TPU:0, one launch (start us, length us, event | category | flops | bytes accessed | tf_op | source)
XLA Modules:
  0.0 104.9 jit_solution(4063734230791442374)
XLA Ops:
  0.6 0.7 convert_element_type.7
  1.3 0.7 convert_bitcast_fusion
  1.9 0.1 pad.3.clone
  2.0 0.1 copy.20
  2.1 0.1 copy.21
  2.2 0.8 copy.19
  2.9 0.7 maximum_maximum_fusion.sens
  3.6 85.6 %shard_map.122 = (f32[64,64,128]{2,1,0:T(8,128)}, f32[4,24,128]{2,1,0:T(8,128)}) custom-call(f32[8]{0:T(128)} %bulk_t.1, f32[8]{0:T(128)} %buoy_t.1, f32[64]{0:T(128)} %grav.1, s32[64,128]{1,0:T(8,128)} %classes.1, f32[8,128]{1,0:T(8,128)} %maximum_maximum_fusion.sens, f32[64,64,128]{2,1,0:T(8,128)} %p_hbm.1, f32[64,64,128]{2,1,0:T(8,128)} %sv_hbm.1, ...), custom_call_target="tpu_custom_call" | custom-call | tf_op jit(solution)/shard_map/pallas_call | solution.py:555
  89.2 0.9 copy.25
  90.1 0.8 fusion
  90.9 8.8 %cholesky.18 = f32[96,96]{1,0:T(8,128)S(1)} custom-call(f32[96,96]{1,0:T(8,128)S(1)} %fusion), custom_call_target="Cholesky" | custom-call | tf_op jit(solution)/shard_map/jit(cholesky)/cholesky | solution.py:569
  99.7 0.6 compare_reduce_fusion
  100.4 0.7 select_bitcast_fusion
  101.0 0.7 copy.24
  101.7 3.2 %copy.27 = f32[64,64,128]{2,1,0:T(8,128)} copy(f32[64,64,128]{2,1,0:T(8,128)} %get-tuple-element.12) | data formatting | bytes 4194304
  (2 shorter events, 0.0 us)

commit v3 on v2

--- a/solution.py
+++ b/solution.py
@@ -74,6 +74,9 @@
     qv,
     edge_a,
     edge_b,
+    inner_a,
+    inner_b,
+    dmat,
     sens_all,
     gram,
     part1,
@@ -276,6 +279,19 @@
     bx[pl.ds(END, 8), :] = rb_hi[...]
     hb[...] = jnp.where(low, rbq_l[...], rbq_r[...])
 
+    gap = lax.broadcasted_iota(jnp.int32, (256, 128), 0) - lax.broadcasted_iota(jnp.int32, (256, 128), 1)
+    gap = (gap + 256) & 127
+    weights = jnp.where(gap == 1, 8.0, 0.0) - jnp.where(gap == 127, 8.0, 0.0)
+    weights = weights - jnp.where(gap == 2, 1.0, 0.0) + jnp.where(gap == 126, 1.0, 0.0)
+    dmat[...] = weights.astype(jnp.bfloat16)
+
+    def product_diff(f):
+        flat = f.reshape(4 * rows, 128)
+        hi = flat.astype(jnp.bfloat16)
+        lo = (flat - hi.astype(jnp.float32)).astype(jnp.bfloat16)
+        both = jnp.concatenate([hi, lo], axis=1)
+        return jnp.dot(both, dmat[...], preferred_element_type=jnp.float32).reshape(4, rows, 128)
+
     def phase_a(k, c):
         each_side(lambda i: halo_copy(k, c, i), "recv")
         base = c * CH
@@ -294,6 +310,8 @@
         d_right = lane_diff(jnp.where(low, own, rq_r[k, c]))
         hv[c] = hv[c] - hb[...] * jnp.where(low, d_left, d_right)
         edge_a[...] = jnp.where(low, d_right, d_left)
+        for g in range(0, CH, 4):
+            inner_a[g : g + 4] = product_diff(pe[pl.ds(base + 1 + g, 4), pl.ds(OFF, rows), :])
 
         def level(j, acc):
             lev = base + j
@@ -306,7 +324,7 @@
             se[lev, ext, :] = se[lev, ext, :] - bx[ext, :] * ds
             own_rows = pl.ds(OFF, rows)
             b = bx[own_rows, :]
-            dd = jnp.where(rim, pltpu.roll(edge_a[...], 124 - 8 * j, 1), lane_diff(pe[lev + 1, own_rows, :]))
+            dd = jnp.where(rim, pltpu.roll(edge_a[...], 124 - 8 * j, 1), inner_a[j])
             v = dv[lev] - b * dd
             dv[lev] = v
             dz = (6.0 * b) * (pe[lev + 2, own_rows, :] - pe[lev, own_rows, :])
@@ -325,6 +343,8 @@
         d_left = lane_diff(jnp.where(low, halo, own))
         d_right = lane_diff(jnp.where(low, own, halo))
         edge_b[...] = jnp.where(low, d_right, d_left)
+        for g in range(0, CH, 4):
+            inner_b[g : g + 4] = product_diff(dv[pl.ds(base + g, 4)])
 
         def level(j, acc):
             lev = base + j
@@ -333,7 +353,7 @@
                 return se[lev, pl.ds(OFF + o, rows), :]
 
             ds = 8.0 * (win(1) - win(-1)) - (win(2) - win(-2))
-            dd = jnp.where(rim, pltpu.roll(edge_b[...], 124 - 8 * j, 1), lane_diff(dv[lev]))
+            dd = jnp.where(rim, pltpu.roll(edge_b[...], 124 - 8 * j, 1), inner_b[j])
             dz = 6.0 * (vv[lev + 2] - vv[lev])
             own_rows = pl.ds(OFF, rows)
             f = pe[lev + 1, own_rows, :] - bk[...] * (ds + dd + dz) + (TIME_STEP * grav[lev]) * vv[lev + 1]
@@ -528,6 +548,9 @@
         vmem(nch, rows, cols),
         vmem(rows, cols),
         vmem(rows, cols),
+        vmem(CH, rows, cols),
+        vmem(CH, rows, cols),
+        vmem(2 * cols, cols, dtype=jnp.bfloat16),
         vmem(nd, 8, cols),
         vmem(nd, share, cols),
         vmem(nd - 1, share, cols),

time: 105 us -> 73.1 us (0.70)
  Pallas kernels: 85.6 us -> 53.4 us
    pallas_call x1, Pallas kernels: 85.6 us -> 53.4 us  [body(): pl.pallas_call(functools.partial(kernel, ns, nd, scale), out_shape=(jax.S...]
where the time goes in v3:
time: 73.1 us; the launch traced here: 72.7 us
  Pallas kernels  53.4 us (73%)
  other arithmetic  12.9 us (18%)
  local copies, waits for them, and re-layouts  5.74 us (8%)
    pallas_call x1, Pallas kernels, body(): pl.pallas_call(functools.partial(kernel, ns, nd, scale), out_shape=(jax.S...  53.4 us
    another operation x3, other arithmetic, body(): return (final, jnp.linalg.cholesky(gram).T)  9.45 us
    unnamed x4, local copies, waits for them, and re-layouts  5.5 us

profile of v3, /device:TPU:0, one launch (start us, length us, event | category | flops | bytes accessed | tf_op | source)
XLA Modules:
  0.0 72.7 jit_solution(17988483175264845893)
XLA Ops:
  0.6 0.7 convert_element_type.7
  1.3 0.7 convert_bitcast_fusion
  1.9 0.1 pad.3.clone
  2.0 0.1 copy.20
  2.1 0.1 copy.21
  2.2 0.8 %copy.19 = f32[4,8]{0,1:T(8,128)S(1)} copy(f32[4,8]{1,0:T(4,128)} %param.18) | data formatting | bytes 256 | tf_op args[7]
  2.9 0.7 maximum_maximum_fusion.sens
  3.6 53.4 %shard_map.122 = (f32[64,64,128]{2,1,0:T(8,128)}, f32[4,24,128]{2,1,0:T(8,128)}) custom-call(f32[8]{0:T(128)} %bulk_t.1, f32[8]{0:T(128)} %buoy_t.1, f32[64]{0:T(128)} %grav.1, s32[64,128]{1,0:T(8,128)} %classes.1, f32[8,128]{1,0:T(8,128)} %maximum_maximum_fusion.sens, f32[64,64,128]{2,1,0:T(8,128)} %p_hbm.1, f32[64,64,128]{2,1,0:T(8,128)} %sv_hbm.1, ...), custom_call_target="tpu_custom_call" | custom-call | tf_op jit(solution)/shard_map/pallas_call | solution.py:578
  57.0 0.9 %copy.25 = f32[96,96]{0,1:T(8,128)S(1)} copy(f32[96,96]{1,0:T(8,128)} %bitcast.11) | data formatting | bytes 73728
  57.9 0.8 %fusion = f32[96,96]{1,0:T(8,128)S(1)} fusion(f32[96,96]{0,1:T(8,128)S(1)} %copy.25, f32[96,128]{1,0:T(8,128)} %bitcast.12), kind=kLoop, calls=%fused_computation.1 | loop fusion | flops 18432 | bytes 110592 | tf_op jit(solution)/shard_map/jit(cholesky)/div | solution.py:592
  58.7 8.8 %cholesky.18 = f32[96,96]{1,0:T(8,128)S(1)} custom-call(f32[96,96]{1,0:T(8,128)S(1)} %fusion), custom_call_target="Cholesky" | custom-call | tf_op jit(solution)/shard_map/jit(cholesky)/cholesky | solution.py:592
  67.5 0.6 compare_reduce_fusion
  68.2 0.7 select_bitcast_fusion
  68.8 0.7 copy.24
  69.5 3.2 %copy.27 = f32[64,64,128]{2,1,0:T(8,128)} copy(f32[64,64,128]{2,1,0:T(8,128)} %get-tuple-element.12) | data formatting | bytes 4194304
  (2 shorter events, 0.0 us)
